TPU v7x, 256 devices: a whole 4x4x8 slice. The times are simulated.
256 devices in a mesh: gx: 32 (over y, z), gy: 8 (over x, core).
Axes of the slice: x: 4, y: 4, z: 8, core: 2. Of those that a mesh axis runs over, the one named last changes fastest.
Arguments:
- load_nodes: float32 [4096, 512], P(('gx', 'gy')), may hold values from -6 to 6
- metric: float32 [4096, 3, 512], P(('gx', 'gy')), may hold values from 0.005 to 0.05
- mass_nodes: float32 [4096, 512], P(('gx', 'gy')), may hold values from 0.1 to 1
- smoother: float32 [10, 10], replicated, may hold values from -0.08 to 1.2, as said below
- element_order: int32 [4096], P(('gx', 'gy')), may hold values from 0 to 15, as said below
Outputs:
- pressure: float32 [4096, 512], P(('gx', 'gy'))
- residual: float32 [4096, 512], P(('gx', 'gy'))
Inputs may be any that keep to these rules, and one draw needn't show every extreme that they name: `element_order`: each aligned block of 16 stored elements holds every brick position once. `smoother`: Symmetric, with a diagonal larger than the sum of the magnitudes of the rest of its row.
All inputs are finite; a program needn't handle non-finite values.
Results may differ from a plain program's by a relative error of at most 0.0008.
Values sent between devices are 32-bit elements; how exact they have to be, the bound alone decides.
A program may use at most 64 MiB of HBM per device.

v0:
```python
import functools

import jax
import jax.numpy as jnp
import ml_dtypes
import numpy as np
from jax import lax
from jax.experimental import pallas as pl
from jax.experimental.pallas import tpu as pltpu
from jax.sharding import PartitionSpec as P

NODES = 8
BF16 = ml_dtypes.bfloat16
MESH = pl.DeviceIdType.MESH


def derivative_table(node_count):
    degree = node_count - 1
    points = np.cos(np.pi * np.arange(node_count) / degree)
    weights = np.ones(node_count)
    weights[0] = 2.0
    weights[-1] = 2.0
    matrix = np.zeros((node_count, node_count))
    for row in range(node_count):
        for col in range(node_count):
            if row != col:
                matrix[row, col] = (
                    weights[row]
                    / weights[col]
                    * (-1.0) ** (row + col)
                    / (points[row] - points[col])
                )
        matrix[row, row] = -np.sum(matrix[row])
    return matrix


def split_const(matrix):
    full = np.asarray(matrix, np.float32)
    high = full.astype(BF16)
    return high, (full - high.astype(np.float32)).astype(BF16)


@functools.lru_cache(None)
def tables():
    node = np.array([7 * i + a for i in range(2) for a in range(8)])
    incidence = {}
    for box in (-1, 0, 1, 2):
        block = np.zeros((10, 16))
        for at in range(16):
            idx = node[at] - 7 * box + 1
            if 0 <= idx < 10:
                block[idx, at] = 1.0
        incidence[box] = block
    uc = np.zeros((24, 4, 16))
    uci = np.zeros((24, 16))
    rv = np.zeros((4, 16, 16))
    rvi = np.zeros((16, 16))
    re = np.zeros((16, 2, 16))
    rei = np.zeros((16, 32))
    ae = np.zeros((2, 16, 24))
    aei = np.zeros((32, 24))
    for at in range(16):
        for slot, box in enumerate((-1, 0, 1, 2)):
            uc[at, slot, :10] = incidence[box][:, at]
            rv[slot, :10, at] = incidence[box][:, at]
        re[at, 0, :10] = incidence[0][:, at]
        re[at, 1, :10] = incidence[1][:, at]
        rei[at, at] = 1.0
        aei[at, at] = 1.0
        for dim, where in enumerate((0, 1, 13, 14)):
            rvi[dim, at] = float(node[at] == where)
            rei[at, 16 + dim] = float(node[at] == where)
    uc[16, 2, 8] = uc[17, 2, 9] = uci[18, 2] = uci[19, 3] = 1.0
    uc[20, 1, 0] = uc[21, 1, 1] = uci[22, 0] = uci[23, 1] = 1.0
    aei[16, 16] = aei[17, 17] = ae[0, 0, 18] = ae[0, 1, 19] = 1.0
    aei[18, 20] = aei[19, 21] = ae[1, 8, 22] = ae[1, 9, 23] = 1.0
    assemble = np.zeros((24, 16))
    assemble[:16] = node[:, None] == node[None, :]
    assemble[16] = node == 14
    assemble[21] = node == 0

    lane = np.arange(256)
    xi = (lane // 128) * 8 + (lane // 8) % 8
    eta = ((lane // 64) % 2) * 8 + lane % 8
    mx, my = [], []
    for side in (16, 20):
        for q in range(4):
            for e in range(16):
                mx.append(side + q)
                my.append(e)
    for side in (16, 20):
        for e in range(16):
            for q in range(4):
                mx.append(e)
                my.append(side + q)
    for sx in (16, 20):
        for sy in (16, 20):
            for qx in range(4):
                for qy in range(4):
                    mx.append(sx + qx)
                    my.append(sy + qy)
    mx, my = np.array(mx), np.array(my)

    def padded(rows, index):
        return np.concatenate([rows[index], np.zeros((64,) + rows.shape[1:])], axis=0)

    allx = np.concatenate([xi, mx])
    ally = np.concatenate([eta, my])
    def kernel_side(index):
        rows = uc.reshape(24, 64)
        return padded(np.concatenate([rows, rows, uci], axis=1), index)

    def sending_side(index):
        rows = re.reshape(16, 32)[index]
        return np.concatenate([rows, rows, rei[index]], axis=1)

    spread_e = [padded(ae[box].T, m).T for m in (mx, my) for box in range(2)]
    spread_k = [rv[box][:, at] for at in (xi, eta) for box in range(4)]
    asm = padded(assemble, allx)[:, xi] * padded(assemble, ally)[:, eta]

    znode = np.array([7 * k + c for k in range(4) for c in range(8)])
    rz = np.zeros((4, 16, 32))
    for block in range(4):
        for at in range(32):
            idx = znode[at] - 7 * block + 1
            if 0 <= idx < 10:
                rz[block, idx, at] = 1.0
    spread_z = [np.concatenate([block] * 4, axis=1) for block in rz]
    rzt = rz.reshape(64, 32).T
    az = (znode[:, None] == znode[None, :]).astype(float)

    d = derivative_table(NODES).astype(np.float32)
    eye8 = np.eye(8)
    dx = np.kron(np.eye(2), np.kron(d.T, eye8))
    dy = np.kron(np.eye(2), np.kron(eye8, d.T))
    dxy_hi, dxy_lo = split_const(np.concatenate([dx, dy], axis=1))
    dz = np.kron(np.eye(4), d)
    dz_hi, dz_lo = split_const(dz)
    dzt_hi, dzt_lo = split_const(dz.T)

    b = lambda m: np.asarray(m, BF16)
    return dict(
        dxy_hi=dxy_hi,
        dxy_lo=dxy_lo,
        dxyt_hi=np.ascontiguousarray(dxy_hi.T),
        dxyt_lo=np.ascontiguousarray(dxy_lo.T),
        dz=np.concatenate([dz_hi, dz_hi, dz_lo], axis=1),
        dzt=np.concatenate([dzt_hi, dzt_hi, dzt_lo], axis=1),
        az=b(np.concatenate([az, az], axis=1)),
        uc=b(np.stack([kernel_side(allx), kernel_side(ally)])),
        rvi=b(np.stack([rvi[:, xi], rvi[:, eta]])),
        re=b(np.stack([sending_side(xi), sending_side(eta)])),
        aei=b(np.stack([padded(aei.T, mx).T, padded(aei.T, my).T])),
        spread_e=b(np.concatenate(spread_e, axis=1)),
        spread_k=b(np.concatenate(spread_k + spread_z, axis=1)),
        rzt=b(np.concatenate([rzt, rzt], axis=1)),
        asm=b(asm),
    )


FETCHED = (
    "order", "smoother", "load", "spread_e", "aei", "re", "spread_k", "rvi", "uc", "rzt",
    "metric", "mass", "dxy_hi", "dxy_lo", "dz", "dxyt_hi", "dxyt_lo", "dzt", "asm", "az",
)


def fdot(left, right):
    return jnp.dot(left, right, preferred_element_type=jnp.float32)


def split(value):
    high = value.astype(jnp.bfloat16)
    low = (value - high.astype(jnp.float32)).astype(jnp.bfloat16)
    return high, low


def right_dot(value, w_hi, w_lo):
    rows = value.shape[0]
    high, low = split(value)
    both = fdot(jnp.concatenate([high, low], axis=0), w_hi)
    return both[:rows] + both[rows:] + fdot(high, w_lo)


def left_dot(stacked, value):
    high, low = split(value)
    return fdot(stacked, jnp.concatenate([high, low, high], axis=0))


def offsets(first, second):
    def far(pair):
        return -min(pair[0], first - pair[0]) - min(pair[1], second - pair[1])

    pairs = [(a, b) for a in range(first) for b in range(second)]
    return sorted(pairs[1:], key=far)


def iota(shape, dim):
    return lax.broadcasted_iota(jnp.int32, shape, dim)


def half_roll(value):
    return pltpu.roll(value, 64, 1)


def local_sum(pairs):
    t = sum(first * second for first, second in pairs)
    t = t[0:8] + t[8:16] + t[16:24] + t[24:32]
    return t[:, :128] + t[:, 128:]


def kernel(
    nx, ny, lo,
    *refs,
):
    count = len(FETCHED)
    far = dict(zip(FETCHED, refs[:count]))
    near = dict(zip(FETCHED, refs[count + 5:2 * count + 5]))
    pressure_ref, residual_ref, direction_ref, image_ref, alpha_ref = refs[count:count + 5]
    (
        fetch_sem, sel, k_hi, k_lo, e_hi, e_lo, s_pad,
        slopes_ref, geometry, tz_ref, own_ref, rows_ref,
        halo_out, halo_in, halo_send, halo_recv,
        plane_in, plane_send, plane_recv, column_in, column_send, column_recv,
    ) = refs[2 * count + 5:]
    gx = lax.axis_index("gx")
    gy = lax.axis_index("gy")
    hi = nx // lo
    x_low, x_high = lax.rem(gx + nx - 1, nx), lax.rem(gx + 1, nx)
    y_low, y_high = lax.rem(gy + ny - 1, ny), lax.rem(gy + 1, ny)
    has_low_x, has_high_x = gx > 0, gx < nx - 1
    has_low_y, has_high_y = gy > 0, gy < ny - 1
    neighbours = (
        ((x_low, gy), 0, has_low_x), ((x_high, gy), 1, has_high_x),
        ((gx, y_low), 2, has_low_y), ((gx, y_high), 3, has_high_y),
        ((x_low, y_low), 4, has_low_x & has_low_y), ((x_low, y_high), 4, has_low_x & has_high_y),
        ((x_high, y_low), 4, has_high_x & has_low_y), ((x_high, y_high), 4, has_high_x & has_high_y),
    )
    inside_x, inside_y = has_low_x & has_high_x, has_low_y & has_high_y
    inside = inside_x & inside_y
    at_corner = jnp.logical_not(inside_x | inside_y)
    at_edge = jnp.logical_not(inside | at_corner)

    def where_there(actions, there):
        @pl.when(inside)
        def _():
            for action in actions:
                action()

        @pl.when(jnp.logical_not(inside))
        def _():
            for action, is_there in zip(actions, there):
                pl.when(is_there)(action)

    filled = [neighbours[at][2] for at in (1, 0, 3, 2, 7, 6, 5, 4)]

    z_at, y_at = lax.rem(gx, lo), lax.div(gx, lo)
    x_at, core = lax.div(gy, 2), lax.rem(gy, 2)
    first_core = core == 0
    sibling = (gx, gy + 1 - 2 * core)
    plane = [
        (lax.rem(y_at + a, hi) * lo + z_at, lax.rem(x_at + b, ny // 2) * 2)
        for a, b in offsets(hi, ny // 2)
    ]
    plane_from = [
        (lax.rem(y_at + hi - a, hi) * lo + z_at, lax.rem(x_at + ny // 2 - b, ny // 2) * 2)
        for a, b in offsets(hi, ny // 2)
    ]
    column = [(y_at * lo + lax.rem(z_at + a, lo), x_at * 2) for a, _ in offsets(lo, 1)]
    column_from = [(y_at * lo + lax.rem(z_at + lo - a, lo), x_at * 2) for a, _ in offsets(lo, 1)]

    barrier = pltpu.get_barrier_semaphore()

    def greet(peer, is_there=None):
        def signal():
            pl.semaphore_signal(barrier, inc=1, device_id=peer, device_id_type=MESH)

        if is_there is None:
            signal()
        else:
            pl.when(is_there)(signal)

    def greet_plane(peers):
        @pl.when(first_core)
        def _():
            for peer_x, peer_y in peers:
                greet((peer_x, peer_y + 1))
                greet((peer_x, peer_y))

    greet_plane(plane_from[:5])
    for peer in column_from[:3]:
        greet(peer)
    for peer, _, is_there in neighbours[::-1]:
        greet(peer, is_there)
    greet_plane(plane_from[5:])
    for peer in column_from[3:]:
        greet(peer)
    greet((gx, gy + 1 - 2 * core))

    heard = len(plane) + jnp.where(first_core, 2 * len(column) + 1, 1)
    for _, _, is_there in neighbours:
        heard = heard + is_there.astype(jnp.int32)

    fetches = {}
    for at, name in enumerate(FETCHED):
        fetches[name] = pltpu.make_async_copy(far[name], near[name], fetch_sem.at[at])
        fetches[name].start()

    def c(name):
        if name in fetches:
            fetches.pop(name).wait()
        return near[name]

    col = iota((64, 512), 1)
    for block in range(8):
        at = iota((64, 512), 0) + block * 64
        sel[block * 64:block * 64 + 64] = (
            ((at & 7) * 64 + (at >> 3)) == col
        ).astype(jnp.float32).astype(jnp.bfloat16)

    lane1 = iota((1, 128), 1)
    order_ref = c("order")
    row16 = iota((16, 128), 0)
    along_lanes = jnp.zeros((1, 128), jnp.int32)
    along_rows = jnp.zeros((16, 128), jnp.int32)
    for at in range(16):
        along_lanes = jnp.where((lane1 & 15) == at, order_ref[at], along_lanes)
        along_rows = jnp.where(row16 == at, order_ref[at], along_rows)
    row = iota((128, 128), 0)
    place = (
        ((row >> 3) == along_lanes) & (((row & 7) >> 1) == ((lane1 & 63) >> 4))
    ).astype(jnp.float32).astype(jnp.bfloat16)
    lane16 = iota((16, 128), 1)
    unplace = jnp.concatenate(
        [((lane16 >> 3) == along_rows) & (((lane16 & 7) >> 1) == u) for u in range(4)], axis=0
    ).astype(jnp.float32).astype(jnp.bfloat16)

    row32 = iota((32, 128), 0)
    lane32 = iota((32, 128), 1)
    parity = row32 & 1
    left_half = lane32 < 64

    def from_rows(fields):
        count = len(fields)
        parts = [split(f) for f in fields]
        stacked = jnp.concatenate([p[0] for p in parts] + [p[1] for p in parts], axis=0)
        moved = fdot(stacked, sel[...]).astype(jnp.bfloat16)
        out = []
        for f in range(count):
            pieces = []
            for part in range(2):
                z = moved[(part * count + f) * 16:(part * count + f) * 16 + 16]
                pieces += [z[:, u * 128:u * 128 + 128] for u in range(4)]
            v = fdot(place, jnp.concatenate(pieces, axis=0))
            tiles = []
            for pair in range(2):
                picked = []
                for odd in range(2):
                    at = (pair * 2 + odd) * 32
                    block = v[at:at + 32]
                    picked.append(jnp.where(parity == odd, block, half_roll(block)))
                tiles.append(jnp.where(left_half, picked[0], picked[1]))
            out.append(jnp.concatenate(tiles, axis=1))
        return out

    def to_rows(values):
        count = len(values)
        highs, lows = [], []
        for value in values:
            blocks = []
            for ij in range(4):
                block = value[:, (ij // 2) * 128:(ij // 2) * 128 + 128]
                block = jnp.where(parity == (ij & 1), block, half_roll(block))
                blocks.append(jnp.where((lane32 >> 6) == parity, block, 0.0))
            high, low = split(jnp.concatenate(blocks, axis=0))
            highs.append(high)
            lows.append(low)
        o = fdot(unplace, jnp.concatenate(highs + lows, axis=1)).astype(jnp.bfloat16)
        rows = []
        for v in range(2 * count):
            rows.append(
                jnp.concatenate(
                    [o[u * 16:u * 16 + 16, v * 128:v * 128 + 128] for u in range(4)], axis=1
                )
            )
        n = lax.dot_general(
            jnp.concatenate(rows, axis=0), sel[...], (((1,), (1,)), ((), ())),
            preferred_element_type=jnp.float32,
        )
        return [
            n[v * 16:v * 16 + 16] + n[(count + v) * 16:(count + v) * 16 + 16]
            for v in range(count)
        ]

    for name in ("smoother", "load", "spread_e", "aei", "re"):
        c(name)
    s_pad[...] = jnp.zeros((16, 128), jnp.float32)
    s_pad[0:10, 0:10] = c("smoother")[...]
    both_parts = jnp.concatenate(split(s_pad[...]), axis=0)[:, 0:16]
    entries = fdot(both_parts, c("spread_e")[...]).astype(jnp.bfloat16)

    def stacked_entries(entries, at, width, number):
        blocks = [entries[:, at + b * width:at + (b + 1) * width] for b in range(number)]
        return [block[0:16] for block in blocks] + [block[16:32] for block in blocks]

    for axis in range(2):
        wide = fdot(
            c("re")[axis],
            jnp.concatenate(
                stacked_entries(entries, axis * 768, 384, 2) + [c("aei")[axis]], axis=0
            ),
        )
        enc = wide if axis == 0 else enc * wide
    high, low = split(enc)
    e_hi[...] = high
    e_lo[...] = low

    r0, = from_rows([c("load")[...]])

    low_x = (gx == 0).astype(jnp.float32)
    high_x = (gx == nx - 1).astype(jnp.float32)
    low_y = (gy == 0).astype(jnp.float32)
    high_y = (gy == ny - 1).astype(jnp.float32)
    left16 = lane16 < 64
    quarter = (lane16 & 63) >> 4

    for slot, is_filled in enumerate(filled):
        @pl.when(jnp.logical_not(is_filled))
        def _():
            for stage in range(4):
                halo_in[stage, slot] = jnp.zeros((16, 128), jnp.float32)

    pl.semaphore_wait(barrier, heard)

    halos = []

    def exchange_start(stage, value):
        m = right_dot(value, e_hi[...], e_lo[...])
        for pair in range(2):
            t = m[:, pair * 128:pair * 128 + 128]
            top, bottom = t[0:16], t[16:32]
            halo_out[stage, 2 * pair] = jnp.where(left16, top, half_roll(bottom))
            halo_out[stage, 2 * pair + 1] = jnp.where(left16, half_roll(top), bottom)
        t = m[:, 256:384]
        halo_out[stage, 4] = jnp.where(left16, t[0:16], half_roll(t[16:32]))
        copies = []
        for slot in (0, 1, 4, 5, 6, 7, 2, 3):
            peer, part, is_there = neighbours[slot]
            copy = pltpu.make_async_remote_copy(
                src_ref=halo_out.at[stage, part],
                dst_ref=halo_in.at[stage, slot],
                send_sem=halo_send.at[stage, slot],
                recv_sem=halo_recv.at[stage],
                device_id=peer,
                device_id_type=MESH,
            )
            copies.append((copy, is_there))
        where_there([copy.start for copy, _ in copies], [there for _, there in copies])
        halos.extend(copies)

    def exchange_end(stage):
        for number, here in ((8, inside), (5, at_edge), (3, at_corner)):
            arrived = halo_in.at[stage, pl.ds(0, number)]
            pl.when(here)(
                pltpu.make_async_remote_copy(
                    src_ref=arrived,
                    dst_ref=arrived,
                    send_sem=halo_send.at[stage, 0],
                    recv_sem=halo_recv.at[stage],
                    device_id=sibling,
                    device_id_type=MESH,
                ).wait_recv
            )
        tiles = []
        for pair in range(2):
            a, b = halo_in[stage, 2 * pair], halo_in[stage, 2 * pair + 1]
            tiles.append(
                jnp.concatenate(
                    [jnp.where(left16, a, half_roll(b)), jnp.where(left16, half_roll(a), b)],
                    axis=0,
                )
            )
        corner = jnp.where(
            quarter == 0, halo_in[stage, 4],
            jnp.where(
                quarter == 1, halo_in[stage, 5],
                jnp.where(quarter == 2, halo_in[stage, 6], halo_in[stage, 7]),
            ),
        )
        tiles.append(jnp.concatenate([corner, half_roll(corner)], axis=0))
        return jnp.concatenate(tiles, axis=1)

    others = 2 * len(plane) + 1

    def plane_copy(which, target, peer, tiles=1):
        source = plane_in.at[which, pl.ds(others, 1)] if tiles == 1 else target
        return pltpu.make_async_remote_copy(
            src_ref=source,
            dst_ref=target,
            send_sem=plane_send.at[which],
            recv_sem=plane_recv.at[which],
            device_id=peer,
            device_id_type=MESH,
        )

    def column_copy(which, target, peer, tiles=1):
        source = column_in.at[which, pl.ds(0, 1)] if tiles == 1 else target
        return pltpu.make_async_remote_copy(
            src_ref=source,
            dst_ref=target,
            send_sem=column_send.at[which],
            recv_sem=column_recv.at[which],
            device_id=peer,
            device_id_type=MESH,
        )

    def tree_sum(parts):
        while len(parts) > 1:
            parts = [sum(parts[at:at + 2]) for at in range(0, len(parts), 2)]
        return parts[0]

    def sum_start(which, value):
        plane_in[which, others] = value
        for at, peer in enumerate(plane):
            plane_copy(which, plane_in.at[which, pl.ds(2 * at + core, 1)], peer).start()

        @pl.when(jnp.logical_not(first_core))
        def _():
            plane_copy(which, plane_in.at[which, pl.ds(others - 1, 1)], sibling).start()

    def sum_middle(which):
        @pl.when(first_core)
        def _():
            arrived = plane_in.at[which, pl.ds(0, others)]
            plane_copy(which, arrived, sibling, others).wait_recv()
            column_in[which, 0] = tree_sum([plane_in[which, slot] for slot in range(others + 1)])
            for at, (peer_x, peer_y) in enumerate(column):
                for other in (1, 0):
                    target = column_in.at[which, pl.ds(at + 1, 1)]
                    column_copy(which, target, (peer_x, peer_y + other)).start()
            column_copy(which, column_in.at[which, pl.ds(0, 1)], sibling).start()

    def sum_end(which):
        @pl.when(first_core)
        def _():
            arrived = column_in.at[which, pl.ds(1, len(column))]
            column_copy(which, arrived, sibling, len(column)).wait_recv()

        @pl.when(jnp.logical_not(first_core))
        def _():
            arrived = column_in.at[which, pl.ds(0, len(column) + 1)]
            column_copy(which, arrived, sibling, len(column) + 1).wait_recv()

        return tree_sum([column_in[which, slot] for slot in range(len(column) + 1)])

    def plane_sent(which):
        @pl.when(first_core)
        def _():
            leaving = plane_in.at[which, pl.ds(0, len(plane))]
            plane_copy(which, leaving, sibling, len(plane)).wait_send()

        @pl.when(jnp.logical_not(first_core))
        def _():
            leaving = plane_in.at[which, pl.ds(0, len(plane) + 1)]
            plane_copy(which, leaving, sibling, len(plane) + 1).wait_send()

    def column_sent(which):
        @pl.when(first_core)
        def _():
            number = 2 * len(column) + 1
            leaving = plane_in.at[which, pl.ds(0, number)]
            column_copy(which, leaving, sibling, number).wait_send()

    row8 = iota((8, 128), 0)

    def partial_tile(pairs):
        tile = jnp.zeros((8, 128), jnp.float32)
        for q, products in enumerate(pairs):
            t = local_sum(products)
            for shift in (4, 2, 1):
                t = t + pltpu.roll(t, shift, 0)
            tile = jnp.where(row8 == q, t, tile)
        return tile

    def scalars(total, number):
        column = jnp.sum(total, axis=1, keepdims=True)
        return [column[q:q + 1] for q in range(number)]

    exchange_start(0, r0)

    for name in ("spread_k", "rvi", "uc", "rzt", "metric", "mass"):
        c(name)
    entries = fdot(both_parts, c("spread_k")[...]).astype(jnp.bfloat16)
    for axis, low_edge, high_edge in ((0, low_x, high_x), (1, low_y, high_y)):
        blocks = stacked_entries(entries, axis * 1024, 256, 4)
        for at in (0, 4):
            blocks[at] = blocks[at] * (1.0 - low_edge).astype(jnp.bfloat16)
            blocks[at + 3] = blocks[at + 3] * (1.0 - high_edge).astype(jnp.bfloat16)
        wide = fdot(c("uc")[axis], jnp.concatenate(blocks + [c("rvi")[axis]], axis=0))
        kxy = wide if axis == 0 else kxy * wide
    high, low = split(kxy)
    k_hi[...] = high
    k_lo[...] = low
    tz = fdot(c("rzt")[...], jnp.concatenate(stacked_entries(entries, 2048, 128, 4), axis=0))
    tz_hi, tz_lo = split(tz[:, 0:96])
    tz = jnp.where(iota((32, 96), 1) < 64, tz_hi.astype(jnp.float32), tz_lo.astype(jnp.float32))
    tz_ref[...] = tz.astype(jnp.bfloat16)

    metric = c("metric")
    m0, m1, m2, mass = from_rows(
        [metric[0], metric[1], metric[2], c("mass")[...]]
    )
    slopes_ref[...] = jnp.concatenate(
        [
            jnp.concatenate([m0[:, :128], m1[:, :128]], axis=1),
            jnp.concatenate([m0[:, 128:], m1[:, 128:]], axis=1),
        ],
        axis=0,
    )

    geometry[0] = m2
    geometry[1] = mass

    def own_part(stage, value):
        own_ref[stage] = right_dot(value, k_hi[0:256], k_lo[0:256])

    def precondition(stage, arrived):
        return left_dot(
            tz_ref[...], own_ref[stage] + right_dot(arrived, k_hi[256:640], k_lo[256:640])
        )

    def slopes(u):
        tall = jnp.concatenate([u[:, :128], u[:, 128:]], axis=0)
        return right_dot(tall, c("dxy_hi")[...], c("dxy_lo")[...]), left_dot(c("dz")[...], u)

    def operate(u, grad):
        slope = slopes_ref[...] * grad[0]
        slope_z = geometry[0] * grad[1]
        tall = right_dot(slope, c("dxyt_hi")[...], c("dxyt_lo")[...])
        return (
            jnp.concatenate([tall[:32], tall[32:]], axis=1)
            + left_dot(c("dzt")[...], slope_z)
            + geometry[1] * u
        )

    def assembled(value, arrived):
        both = jnp.concatenate([value, arrived], axis=1)
        high, low = split(both)
        t = fdot(jnp.concatenate([high, low], axis=0), c("asm")[...])
        t = t[:32] + t[32:]
        high, low = split(t)
        return fdot(c("az")[...], jnp.concatenate([high, low], axis=0))

    own_part(0, r0)
    for name in ("dxy_hi", "dxy_lo", "dz", "dxyt_hi", "dxyt_lo", "dzt", "asm", "az"):
        c(name)
    arrived_r0 = exchange_end(0)
    z0 = precondition(0, arrived_r0)
    w0 = operate(z0, slopes(z0))

    exchange_start(1, w0)
    sum_start(0, partial_tile([[(r0, z0)], [(w0, z0)]]))
    own_part(1, w0)
    arrived_w0 = exchange_end(1)
    z1 = precondition(1, arrived_w0)
    grad1 = slopes(z1)
    w1 = operate(z1, grad1)
    exchange_start(2, w1)
    sum_middle(0)
    own_part(2, w1)
    for at, value in enumerate(
        to_rows([z0, z1, assembled(r0, arrived_r0), assembled(w0, arrived_w0)])
    ):
        rows_ref[at] = value
    arrived_w1 = exchange_end(2)
    z2 = precondition(2, arrived_w1)
    grad2 = slopes(z2)
    gamma0, delta0 = scalars(sum_end(0), 2)
    alpha0 = gamma0 / delta0
    per_gamma0 = 1.0 / gamma0
    per_alpha0 = delta0 / gamma0

    r1 = r0 - alpha0 * w0
    u1 = z0 - alpha0 * z1
    v1 = w0 - alpha0 * w1
    q = z1 - alpha0 * z2
    grad_q = grad1[0] - alpha0 * grad2[0]
    grad_qz = grad1[1] - alpha0 * grad2[1]
    slope_q = slopes_ref[...] * grad_q
    sum_start(
        1,
        partial_tile(
            [
                [(r1, u1)], [(v1, u1)], [(v1, q)], [(v1, z1)], [(w0, z1)],
                [
                    (slope_q[:32], grad_q[:32]), (slope_q[32:], grad_q[32:]),
                    (geometry[0] * grad_qz, grad_qz), (geometry[1] * q, q),
                ],
                [(w1, q)], [(w1, z1)],
            ]
        ),
    )
    w2 = operate(z2, grad2)
    exchange_start(3, w2)
    for at, value in enumerate(to_rows([z2, assembled(w1, arrived_w1)])):
        rows_ref[4 + at] = value
    sum_middle(1)
    arrived_w2 = exchange_end(3)
    rows_w2, = to_rows([assembled(w2, arrived_w2)])
    rows_z0, rows_z1, rows_r0, rows_w0, rows_z2, rows_w1 = [rows_ref[at] for at in range(6)]
    rows_ref[1] = rows_z0 - alpha0 * rows_z1
    rows_ref[4] = rows_z1 - alpha0 * rows_z2
    rows_ref[2] = rows_r0 - alpha0 * rows_w0
    rows_ref[5] = rows_w0 - alpha0 * rows_w1
    rows_ref[6] = rows_w1 - alpha0 * rows_w2
    pressure_ref[...] = rows_z1
    residual_ref[...] = rows_w1
    where_there([copy.wait_send for copy, _ in halos], [there for _, there in halos])
    plane_sent(0)
    plane_sent(1)
    column_sent(0)
    gamma1, delta1, vq, vz, wz0, yq, yz, wz1 = scalars(sum_end(1), 8)

    beta1 = gamma1 * per_gamma0
    uz = -gamma1 * per_alpha0
    curve1 = delta1 + beta1 * uz
    alpha1 = gamma1 / curve1
    per_gamma1 = 1.0 / gamma1
    gamma2 = (
        gamma1 - 2.0 * alpha1 * (delta1 + beta1 * uz)
        + alpha1 * alpha1 * (vq + beta1 * (2.0 * vz + beta1 * wz0))
    )
    delta2 = (
        delta1 - 2.0 * alpha1 * (vq + beta1 * vz)
        + alpha1 * alpha1 * (yq + beta1 * (2.0 * yz + beta1 * wz1))
    )
    beta2 = gamma2 * per_gamma1
    alpha2 = gamma2 / (delta2 - beta2 * gamma2 * (curve1 * per_gamma1))
    rows_z0, rows_u1, rows_r1, rows_w0, rows_q, rows_v1, rows_y = [
        rows_ref[at] for at in range(7)
    ]
    rows_p1 = rows_u1 + beta1 * rows_z0
    rows_u2 = rows_u1 - alpha1 * (rows_q + beta1 * pressure_ref[...])
    rows_s1 = rows_v1 + beta1 * rows_w0
    rows_v2 = rows_v1 - alpha1 * (rows_y + beta1 * residual_ref[...])
    pressure_ref[...] = alpha0 * rows_z0 + alpha1 * rows_p1
    residual_ref[...] = rows_r1 - alpha1 * rows_s1
    direction_ref[...] = rows_u2 + beta2 * rows_p1
    image_ref[...] = rows_v2 + beta2 * rows_s1
    alpha_ref[...] = jnp.broadcast_to(alpha2, (1, 512))
    column_sent(1)


def solution(mesh):
    nx, ny = mesh.shape["gx"], mesh.shape["gy"]
    lo = 8 if nx % 8 == 0 else 2
    consts = tables()
    vmem = pl.BlockSpec(memory_space=pltpu.VMEM)
    rows = jax.ShapeDtypeStruct((16, 512), jnp.float32)
    chips = nx // lo * (ny // 2)
    shapes = dict(
        consts,
        load=rows,
        metric=jax.ShapeDtypeStruct((3, 16, 512), jnp.float32),
        mass=rows,
        smoother=jax.ShapeDtypeStruct((10, 10), jnp.float32),
        order=jax.ShapeDtypeStruct((16,), jnp.int32),
    )
    call = pl.pallas_call(
        functools.partial(kernel, nx, ny, lo),
        out_shape=(pltpu.VMEM((16, 512), jnp.float32),) * 4 + (pltpu.VMEM((1, 512), jnp.float32),),
        in_specs=[pl.BlockSpec(memory_space=pltpu.HBM)] * len(FETCHED),
        out_specs=(vmem,) * 5,
        scratch_shapes=[
            (pltpu.SMEM if name == "order" else pltpu.VMEM)(shapes[name].shape, shapes[name].dtype)
            for name in FETCHED
        ]
        + [
            pltpu.SemaphoreType.DMA((len(FETCHED),)),
            pltpu.VMEM((512, 512), jnp.bfloat16),
            pltpu.VMEM((640, 256), jnp.bfloat16),
            pltpu.VMEM((640, 256), jnp.bfloat16),
            pltpu.VMEM((256, 384), jnp.bfloat16),
            pltpu.VMEM((256, 384), jnp.bfloat16),
            pltpu.VMEM((16, 128), jnp.float32),
            pltpu.VMEM((64, 256), jnp.float32),
            pltpu.VMEM((2, 32, 256), jnp.float32),
            pltpu.VMEM((32, 96), jnp.bfloat16),
            pltpu.VMEM((3, 32, 256), jnp.float32),
            pltpu.VMEM((7, 16, 512), jnp.float32),
            pltpu.VMEM((4, 5, 16, 128), jnp.float32),
            pltpu.VMEM((4, 8, 16, 128), jnp.float32),
            pltpu.SemaphoreType.DMA((4, 8)),
            pltpu.SemaphoreType.DMA((4,)),
            pltpu.VMEM((2, 2 * chips, 8, 128), jnp.float32),
            pltpu.SemaphoreType.DMA((2,)),
            pltpu.SemaphoreType.DMA((2,)),
            pltpu.VMEM((2, lo, 8, 128), jnp.float32),
            pltpu.SemaphoreType.DMA((2,)),
            pltpu.SemaphoreType.DMA((2,)),
        ],
        compiler_params=pltpu.CompilerParams(
            collective_id=0, has_side_effects=True, vmem_limit_bytes=60 * 1024 * 1024
        ),
    )

    def on_device(load_nodes, metric, mass_nodes, smoother, element_order):
        given = dict(
            consts, load=load_nodes, metric=metric.transpose(1, 0, 2), mass=mass_nodes, smoother=smoother,
            order=element_order,
        )
        pressure, residual, direction, image, alpha = call(
            *[jnp.asarray(given[name]) for name in FETCHED]
        )
        return pressure + alpha * direction, residual - alpha * image

    return jax.shard_map(
        on_device,
        mesh=mesh,
        in_specs=(
            P(("gx", "gy"), None),
            P(("gx", "gy"), None, None),
            P(("gx", "gy"), None),
            P(),
            P(("gx", "gy")),
        ),
        out_specs=(P(("gx", "gy"), None), P(("gx", "gy"), None)),
        check_vma=False,
    )
```

profile of v0, /device:TPU:1, one launch (start us, length us, event | category | flops | bytes accessed | tf_op | source)
XLA Modules:
  0.0 37.4 jit_solution(15807938906569612474)
XLA Ops:
  0.6 36.1 %shard_map.203 = (f32[16,512]{1,0:T(8,128)S(1)}, f32[16,512]{1,0:T(8,128)S(1)}, f32[16,512]{1,0:T(8,128)S(1)}, f32[16,512]{1,0:T(8,128)S(1)}, f32[1,512]{1,0:T(1,128)S(1)}) custom-call(s32[16]{0:T(128)} %refs_0_.1, f32[10,10]{1,0:T(8,128)} %refs_1_.1, f32[16,512]{1,0:T(8,128)} %refs_2_.1, bf16[16,1536]{1,0:T(8,128)(2,1)} %constant.30.clone.refs_3_, ...), custom_call_target="tpu_custom_call" | custom-call | tf_op jit(solution)/shard_map/pallas_call | solution.py:811
  36.7 0.6 %multiply_subtract_fusion = (f32[16,512]{1,0:T(8,128)}, f32[16,512]{1,0:T(8,128)}) fusion(f32[16,512]{1,0:T(8,128)S(1)} %get-tuple-element.10, f32[16,512]{1,0:T(8,128)S(1)} %get-tuple-element.11, f32[512]{0:T(512)S(1)} %bitcast.2, f32[16,512]{1,0:T(8,128)S(1)} %get-tuple-element.7, f32[16,512]{1,0:T(8,128)S(1)} %get-tuple-element.9), kind=kLoop, calls=%fused_computation | loop fusion | flops 32768 | bytes 198656 | tf_op jit(solution)/shard_map/sub | solution.py:814
where the time goes:
time: 37.5 us; the launch traced here: 37.4 us
  Pallas kernels  36.1 us (96%)
  other arithmetic  0.64 us (2%)
  between operations  0.64 us (2%)
    pallas_call x1, Pallas kernels, on_device(): call(*[jnp.asarray(given[name]) for name in FETCHED])  36.1 us

commit v1 on v0

--- a/solution.py
+++ b/solution.py
@@ -270,31 +270,23 @@
 
     barrier = pltpu.get_barrier_semaphore()
 
-    def greet(peer, is_there=None):
-        def signal():
-            pl.semaphore_signal(barrier, inc=1, device_id=peer, device_id_type=MESH)
-
-        if is_there is None:
-            signal()
-        else:
-            pl.when(is_there)(signal)
-
-    def greet_plane(peers):
-        @pl.when(first_core)
-        def _():
-            for peer_x, peer_y in peers:
-                greet((peer_x, peer_y + 1))
-                greet((peer_x, peer_y))
-
-    greet_plane(plane_from[:5])
-    for peer in column_from[:3]:
+    def greet(peer):
+        pl.semaphore_signal(barrier, inc=1, device_id=peer, device_id_type=MESH)
+
+    where_there(
+        [functools.partial(greet, peer) for peer, _, _ in neighbours[::-1]],
+        [is_there for _, _, is_there in neighbours[::-1]],
+    )
+    for peer in column_from:
         greet(peer)
-    for peer, _, is_there in neighbours[::-1]:
-        greet(peer, is_there)
-    greet_plane(plane_from[5:])
-    for peer in column_from[3:]:
-        greet(peer)
-    greet((gx, gy + 1 - 2 * core))
+
+    @pl.when(first_core)
+    def _():
+        for peer_x, peer_y in plane_from:
+            greet((peer_x, peer_y + 1))
+            greet((peer_x, peer_y))
+
+    greet(sibling)
 
     heard = len(plane) + jnp.where(first_core, 2 * len(column) + 1, 1)
     for _, _, is_there in neighbours:
@@ -423,15 +415,15 @@
     left16 = lane16 < 64
     quarter = (lane16 & 63) >> 4
 
-    for slot, is_filled in enumerate(filled):
-        @pl.when(jnp.logical_not(is_filled))
-        def _():
-            for stage in range(4):
-                halo_in[stage, slot] = jnp.zeros((16, 128), jnp.float32)
+    @pl.when(jnp.logical_not(inside))
+    def _():
+        for slot, is_filled in enumerate(filled):
+            @pl.when(jnp.logical_not(is_filled))
+            def _():
+                for stage in range(4):
+                    halo_in[stage, slot] = jnp.zeros((16, 128), jnp.float32)
 
     pl.semaphore_wait(barrier, heard)
-
-    halos = []
 
     def exchange_start(stage, value):
         m = right_dot(value, e_hi[...], e_lo[...])
@@ -448,28 +440,29 @@
             copy = pltpu.make_async_remote_copy(
                 src_ref=halo_out.at[stage, part],
                 dst_ref=halo_in.at[stage, slot],
-                send_sem=halo_send.at[stage, slot],
+                send_sem=halo_send.at[stage],
                 recv_sem=halo_recv.at[stage],
                 device_id=peer,
                 device_id_type=MESH,
             )
             copies.append((copy, is_there))
         where_there([copy.start for copy, _ in copies], [there for _, there in copies])
-        halos.extend(copies)
+
+    def halo_wait(stage, receiving):
+        for number, here in ((8, inside), (5, at_edge), (3, at_corner)):
+            moved = halo_in.at[stage, pl.ds(0, number)]
+            copy = pltpu.make_async_remote_copy(
+                src_ref=moved,
+                dst_ref=moved,
+                send_sem=halo_send.at[stage],
+                recv_sem=halo_recv.at[stage],
+                device_id=sibling,
+                device_id_type=MESH,
+            )
+            pl.when(here)(copy.wait_recv if receiving else copy.wait_send)
 
     def exchange_end(stage):
-        for number, here in ((8, inside), (5, at_edge), (3, at_corner)):
-            arrived = halo_in.at[stage, pl.ds(0, number)]
-            pl.when(here)(
-                pltpu.make_async_remote_copy(
-                    src_ref=arrived,
-                    dst_ref=arrived,
-                    send_sem=halo_send.at[stage, 0],
-                    recv_sem=halo_recv.at[stage],
-                    device_id=sibling,
-                    device_id_type=MESH,
-                ).wait_recv
-            )
+        halo_wait(stage, True)
         tiles = []
         for pair in range(2):
             a, b = halo_in[stage, 2 * pair], halo_in[stage, 2 * pair + 1]
@@ -714,7 +707,8 @@
     rows_ref[6] = rows_w1 - alpha0 * rows_w2
     pressure_ref[...] = rows_z1
     residual_ref[...] = rows_w1
-    where_there([copy.wait_send for copy, _ in halos], [there for _, there in halos])
+    for stage in range(4):
+        halo_wait(stage, False)
     plane_sent(0)
     plane_sent(1)
     column_sent(0)
@@ -789,7 +783,7 @@
             pltpu.VMEM((7, 16, 512), jnp.float32),
             pltpu.VMEM((4, 5, 16, 128), jnp.float32),
             pltpu.VMEM((4, 8, 16, 128), jnp.float32),
-            pltpu.SemaphoreType.DMA((4, 8)),
+            pltpu.SemaphoreType.DMA((4,)),
             pltpu.SemaphoreType.DMA((4,)),
             pltpu.VMEM((2, 2 * chips, 8, 128), jnp.float32),
             pltpu.SemaphoreType.DMA((2,)),

time: 37.5 us -> 37.2 us (level)
  no operation moved by 1% of the time
where the time goes in v1:
time: 37.2 us; the launch traced here: 37.1 us
  Pallas kernels  35.8 us (96%)
  other arithmetic  0.64 us (2%)
  between operations  0.64 us (2%)
    pallas_call x1, Pallas kernels, on_device(): call(*[jnp.asarray(given[name]) for name in FETCHED])  35.8 us

profile of v1, /device:TPU:1, one launch (start us, length us, event | category | flops | bytes accessed | tf_op | source)
XLA Modules:
  0.0 37.1 jit_solution(14222204057140532695)
XLA Ops:
  0.6 35.8 %shard_map.203 = (f32[16,512]{1,0:T(8,128)S(1)}, f32[16,512]{1,0:T(8,128)S(1)}, f32[16,512]{1,0:T(8,128)S(1)}, f32[16,512]{1,0:T(8,128)S(1)}, f32[1,512]{1,0:T(1,128)S(1)}) custom-call(s32[16]{0:T(128)} %refs_0_.1, f32[10,10]{1,0:T(8,128)} %refs_1_.1, f32[16,512]{1,0:T(8,128)} %refs_2_.1, bf16[16,1536]{1,0:T(8,128)(2,1)} %constant.30.clone.refs_3_, ...), custom_call_target="tpu_custom_call" | custom-call | tf_op jit(solution)/shard_map/pallas_call | solution.py:805
  36.5 0.6 %multiply_subtract_fusion = (f32[16,512]{1,0:T(8,128)}, f32[16,512]{1,0:T(8,128)}) fusion(f32[16,512]{1,0:T(8,128)S(1)} %get-tuple-element.10, f32[16,512]{1,0:T(8,128)S(1)} %get-tuple-element.11, f32[512]{0:T(512)S(1)} %bitcast.2, f32[16,512]{1,0:T(8,128)S(1)} %get-tuple-element.7, f32[16,512]{1,0:T(8,128)S(1)} %get-tuple-element.9), kind=kLoop, calls=%fused_computation | loop fusion | flops 32768 | bytes 198656 | tf_op jit(solution)/shard_map/sub | solution.py:808
